TPU v7x, 32 devices: a whole 2x2x4 slice. The times are simulated.
32 devices in a mesh: blk: 8 (over y, x, core), dom: 4 (over z).
Axes of the slice: x: 2, y: 2, z: 4, core: 2. Of those that a mesh axis runs over, the one named last changes fastest.
Arguments:
- pno_basis: float32 [256, 64, 256], P(('blk', 'dom')), may hold values from -0.375 to 0.375
- amplitudes: float32 [256, 4096], P(('blk', 'dom')), may hold values from -6 to 6
- send_list: int32 [8, 4, 8, 1], P('blk', 'dom'), may hold values from 0 to 7
- couple: int32 [256, 8], P(('blk', 'dom')), may hold values from 0 to 7, as said below
- couple_weight: float32 [256, 8], P(('blk', 'dom')), may hold values from 0.25 to 1
- fit_weight: float32 [256, 16], P(('blk', 'dom')), may hold values from 0.25 to 1
- fit_blocks: float32 [16, 2, 256, 256], P('blk', None, 'dom'), may hold values from -0.375 to 0.375
Outputs:
- updated: float32 [256, 4096], P(('blk', 'dom'))
Inputs may be any that keep to these rules, and one draw needn't show every extreme that they name: `couple`: slot j of a device holds what peer j // 1 of blk sent it in its place j % 1; on every device each slot is named by at least one coupling.
All inputs are finite; a program needn't handle non-finite values.
Results may differ from a plain program's by a relative error of at most 0.0003.
Values sent between devices are 32-bit elements; how exact they have to be, the bound alone decides.
No kernel may reach another device: no remote copies, remote signals or barrier semaphores. Data moves between devices by JAX's collectives and lax.ppermute only.
A program may use at most 64 MiB of HBM per device.

v0:
```python
import jax
import jax.numpy as jnp
from jax import lax
from jax.experimental import pallas as pl
from jax.experimental.pallas import tpu as pltpu
from jax.sharding import PartitionSpec as P

HIGHEST = lax.Precision.HIGHEST
SET = 4
NN = (((1,), (0,)), ((), ()))
NT = (((1,), (1,)), ((), ()))


def halves(x):
    high = x.astype(jnp.bfloat16)
    return high, (x - high.astype(jnp.float32)).astype(jnp.bfloat16)


def dot(a, b, dims):
    return lax.dot_general(a, b, dims, preferred_element_type=jnp.float32)


def dot3(a, b, dims):
    (a_high, a_low), (b_high, b_low) = a, b
    return dot(a_high, b_high, dims) + (dot(a_high, b_low, dims) + dot(a_low, b_high, dims))


def stack(parts, axis=0):
    return jnp.concatenate(parts, axis=axis)


def from_partner(x, axis, flip):
    return lax.ppermute(x, axis, [(i, i ^ flip) for i in range(lax.axis_size(axis))])


def from_behind(x, axis, by):
    count = lax.axis_size(axis)
    return lax.ppermute(x, axis, [(i, (i + by) % count) for i in range(count)])


def vmem(count):
    return [pl.BlockSpec(memory_space=pltpu.VMEM)] * count


def pack_kernel(send, basis, amps, out):
    pno_count = amps.shape[1]
    lanes = basis.shape[2] // pno_count
    step = pno_count // lanes
    for peer in range(out.shape[0]):
        pair = send[peer]
        out[peer, :pno_count] = basis[pair]
        listed = amps[pair]
        out[peer, pno_count:] = stack([listed[i * step:(i + 1) * step] for i in range(lanes)], 1)


def pack_pairs(send_order, basis, amps):
    _, pno_count, orbital_count = basis.shape
    rows = pno_count + pno_count * pno_count // orbital_count
    return pl.pallas_call(
        pack_kernel,
        out_shape=jax.ShapeDtypeStruct((send_order.shape[0], rows, orbital_count), jnp.float32),
        in_specs=[pl.BlockSpec(memory_space=pltpu.SMEM), *vmem(2)],
        out_specs=vmem(1)[0],
        compiler_params=pltpu.CompilerParams(vmem_limit_bytes=4 * 2**20),
        cost_estimate=pl.CostEstimate(flops=0, bytes_accessed=4 * basis.size, transcendentals=0),
    )(send_order, basis, amps)


def dress_kernel(couple, couple_weight, fit_weight, basis, amps, coupled, dressed, result, turned):
    pair_count, pno_count, orbital_count = basis.shape
    half = pno_count // 2
    slot_count = coupled.shape[0]
    own = halves(basis[...].reshape(pair_count * pno_count, orbital_count))
    others = halves(coupled[:, :pno_count].reshape(slot_count * pno_count, orbital_count))
    overlap = halves(dot3(own, others, NT))
    left, slot_weight = [], []
    for slot in range(slot_count):
        cols = slice(slot * pno_count, (slot + 1) * pno_count)
        packed = coupled[slot, pno_count:]
        partner = stack([packed[:, i:i + pno_count] for i in range(0, orbital_count, pno_count)])
        left.append(dot3([x[:, cols] for x in overlap], halves(partner), NN))
        named = jnp.where(couple[...] == slot, couple_weight[...], 0.0)
        slot_weight.append(jnp.sum(named, axis=1, keepdims=True))
    dressed[:, half:, :] = jnp.zeros((pair_count, dressed.shape[1] - half, 2 * pno_count), jnp.float32)
    for pair in range(pair_count):
        rows = slice(pair * pno_count, (pair + 1) * pno_count)
        scaled = stack([x[rows] * w[pair:pair + 1] for x, w in zip(left, slot_weight)], 1)
        total = amps[pair] + dot3(halves(scaled), [x[rows] for x in overlap], NT)
        dressed[pair, :half] = stack([total[:half], total[half:]], 1)
        turned[pair] = total
        result[pair] = two_to_one(turned, pair, half)
        dressed[pair, half:half + 1, : fit_weight.shape[1]] = fit_weight[pair:pair + 1, :]


def two_to_one(ref, pair, half):
    return stack([ref[pair, pl.ds(i, half, stride=2), :] for i in range(2)], 1)


def dress(couple, couple_weight, fit_weight, basis, amps, coupled):
    pair_count, pno_count, _ = basis.shape
    return pl.pallas_call(
        dress_kernel,
        out_shape=tuple(
            jax.ShapeDtypeStruct((pair_count, pno_count // 2 + more, 2 * pno_count), jnp.float32) for more in (8, 0)
        ),
        in_specs=vmem(6),
        out_specs=tuple(vmem(2)),
        scratch_shapes=[pltpu.VMEM((pair_count, pno_count, pno_count), jnp.float32)],
        compiler_params=pltpu.CompilerParams(vmem_limit_bytes=10 * 2**20),
        cost_estimate=pl.CostEstimate(flops=4 * 10**9, bytes_accessed=8 * basis.size, transcendentals=0),
    )(couple, couple_weight, fit_weight, basis, amps, coupled)


def fold(x):
    return x + pltpu.roll(x, x.shape[1] // 2, 1)


def left_lanes(x):
    return lax.broadcasted_iota(jnp.int32, x.shape, 1) < x.shape[1] // 2


def split(x):
    high = x.astype(jnp.bfloat16)
    wide = high.astype(jnp.float32)
    return high, wide, x - wide


def high_low(x):
    _, high, low = split(x)
    return jnp.where(left_lanes(x), high, low).astype(jnp.bfloat16)


def split_blocks(pieces, block_cat):
    dom_count = len(pieces)
    block_count, part_count, row_count, orbital_count = pieces[0].shape
    place = lax.axis_index("dom")
    for shift, piece in enumerate(pieces):
        start = lax.rem(place + dom_count - shift, dom_count) * row_count
        for b in range(block_count):
            for m in range(part_count):
                high, low = halves(piece[b, m])
                for i, x in enumerate((high, high, low)):
                    at = pl.multiple_of(start + i * orbital_count, row_count)
                    block_cat[m, b, pl.ds(at, row_count), :] = x


def split_basis(basis, wide):
    orbital_count = basis.shape[2]
    high, low = halves(basis[...])
    for i, x in enumerate((high, low, high)):
        wide[:, :, i * orbital_count:(i + 1) * orbital_count] = x


def project_member(wide, block_cat, projected, inner_left, inner_right, first_pair):
    pair_count, pno_count, _ = wide.shape
    part_count, block_count, _, orbital_count = block_cat.shape
    size = block_count * pno_count
    basis = wide[...].reshape(pair_count * pno_count, 3 * orbital_count)
    for m in range(part_count):
        for b in range(block_count):
            product = halves(dot(basis, block_cat[m, b], NN).reshape(pair_count, pno_count, orbital_count))
            at = (m * block_count + b) * pno_count
            for i in range(2):
                projected[:, at:at + pno_count, i * orbital_count:(i + 1) * orbital_count] = product[i]
    for pair in range(pair_count):
        here = first_pair + pair
        both = stack([wide[pair, :, i * orbital_count:(i + 1) * orbital_count] for i in range(2)])
        product = [projected[pair, :, i * orbital_count:(i + 1) * orbital_count] for i in range(2)]
        inner = fold(dot(product[0], both, NT) + dot(product[1], both, NT))
        inner_left[here] = high_low(inner[:size])
        high, _, low = split(inner[size:])
        low = jnp.where(left_lanes(low), low, 0.0).astype(jnp.bfloat16)
        for b in range(block_count):
            rows = slice(b * pno_count, (b + 1) * pno_count)
            lanes = slice(b * 2 * pno_count, (b + 1) * 2 * pno_count)
            inner_right[here, :pno_count, lanes] = high[rows]
            inner_right[here, pno_count:, lanes] = low[rows]


def project_all(bases, pieces, inner_left, inner_right, scratch):
    block_cat, wide, projected = scratch
    pair_count = bases[0].shape[0]
    split_blocks(pieces, block_cat)
    for member, basis in enumerate(bases):
        slot = member % 2
        split_basis(basis, wide.at[slot])
        project_member(
            wide.at[slot], block_cat, projected.at[slot], inner_left, inner_right, member * pair_count
        )


def project_kernel(member_count, *refs):
    bases, refs = refs[:member_count], refs[member_count:]
    *pieces, inner_left, inner_right = refs[:-3]
    project_all(bases, pieces, inner_left, inner_right, refs[-3:])


def inner_shapes(pairs, pno_count, block_count):
    return (
        ((pairs, block_count * pno_count, 2 * pno_count), jnp.bfloat16),
        ((pairs, 2 * pno_count, block_count * 2 * pno_count), jnp.bfloat16),
    )


def project_scratch(bases, pieces):
    pair_count, pno_count, _ = bases[0].shape
    block_count, part_count, _, orbital_count = pieces[0].shape
    return [
        pltpu.VMEM((part_count, block_count, 3 * orbital_count, orbital_count), jnp.bfloat16),
        pltpu.VMEM((2, pair_count, pno_count, 3 * orbital_count), jnp.bfloat16),
        pltpu.VMEM((2, pair_count, part_count * block_count * pno_count, 2 * orbital_count), jnp.bfloat16),
    ]


def project_flops(bases, pieces):
    pair_count, pno_count, _ = bases[0].shape
    block_count, part_count, _, orbital_count = pieces[0].shape
    rows = len(bases) * pair_count * pno_count * block_count * part_count
    return 6 * rows * orbital_count * (orbital_count + pno_count)


def project(bases, pieces):
    pair_count, pno_count, _ = bases[0].shape
    shapes = inner_shapes(len(bases) * pair_count, pno_count, pieces[0].shape[0])
    return pl.pallas_call(
        lambda *refs: project_kernel(len(bases), *refs),
        out_shape=tuple(jax.ShapeDtypeStruct(*x) for x in shapes),
        in_specs=vmem(len(bases) + len(pieces)),
        out_specs=tuple(vmem(2)),
        scratch_shapes=project_scratch(bases, pieces),
        compiler_params=pltpu.CompilerParams(vmem_limit_bytes=20 * 2**20),
        cost_estimate=pl.CostEstimate(flops=project_flops(bases, pieces), bytes_accessed=2**20, transcendentals=0),
    )(*bases, *pieces)


def finish_kernel(members, group_count, dom_count, *refs):
    count = len(members)
    groups, refs = refs[:2 * group_count], refs[2 * group_count:]
    bases, pieces, refs = refs[:count], refs[count:count + dom_count], refs[count + dom_count:]
    dressed, after, scratch = refs[:count], refs[count:2 * count], refs[2 * count:]
    inner_left, inner_right, square, moved, total = scratch[:5]
    project_all(bases, pieces, inner_left, inner_right, scratch[5:])
    groups = [*groups, inner_left, inner_right]
    group_count += 1
    pair_count, _, lane_count = dressed[0].shape
    pno_count = lane_count // 2
    half = pno_count // 2
    block_count = inner_left.shape[1] // pno_count
    group_total = lax.axis_size("blk")
    me = lax.axis_index("blk")
    pairs = [(index, pair) for index in range(count) for pair in range(pair_count)]

    def row_of(group, at):
        full = group < group_count - 1
        return members[at // pair_count] * pair_count + at % pair_count if full else at

    weights = []
    for index, member in enumerate(members):
        row = dressed[index][:, half:half + 1, :]
        lane = lax.broadcasted_iota(jnp.int32, row.shape, 2)
        for group in range(group_count):
            stop = lax.rem((me ^ member) + 2 * group_total + group * SET - me, group_total)
            for b in range(block_count):
                kept = jnp.where(lane == stop * block_count + b, row, 0.0)
                weights.append(jnp.sum(kept, axis=2, keepdims=True))
    for at, (index, pair) in enumerate(pairs):
        packed = dressed[index][pair, :half]
        other = pltpu.roll(packed, pno_count, 1)
        keep = left_lanes(packed)
        _, high, low = split(stack([jnp.where(keep, packed, other), jnp.where(keep, other, packed)]))
        square[at, :pno_count] = jnp.where(left_lanes(low), high, low).astype(jnp.bfloat16)
        square[at, pno_count:] = jnp.where(left_lanes(low), high, 0.0).astype(jnp.bfloat16)
    for at, (index, pair) in enumerate(pairs):
        for group in range(group_count):
            product = fold(dot(groups[2 * group][row_of(group, at)], square[at], NN))
            for b in range(block_count):
                weight = weights[(index * group_count + group) * block_count + b][pair]
                lanes = slice(b * lane_count, (b + 1) * lane_count)
                moved[at, group, :, lanes] = high_low(product[b * pno_count:(b + 1) * pno_count] * weight)
    for at, (index, pair) in enumerate(pairs):
        terms = [dot(moved[at, group], groups[2 * group + 1][row_of(group, at)], NT) for group in range(group_count)]
        total[at] = fold(sum(terms[1:], terms[0]))
    for at, (index, pair) in enumerate(pairs):
        rows = [total[at, pl.ds(i, half, stride=2), :] for i in range(2)]
        after[index][pair] = jnp.where(left_lanes(rows[0]), *rows)


def finish(members, groups, bases, pieces, dressed):
    pair_count, _, lane_count = dressed[0].shape
    pno_count = lane_count // 2
    pairs = len(members) * pair_count
    group_count = len(groups)
    block_count = pieces[0].shape[0]
    operands = [x for group in groups for x in group] + bases + pieces + dressed
    products = pairs * pno_count**3 * 2 * (group_count + 1) * block_count
    shapes = inner_shapes(pairs, pno_count, block_count)
    return pl.pallas_call(
        lambda *refs: finish_kernel(members, group_count, len(pieces), *refs),
        out_shape=[jax.ShapeDtypeStruct((pair_count, pno_count // 2, lane_count), jnp.float32)] * len(members),
        in_specs=vmem(len(operands)),
        out_specs=vmem(len(members)),
        scratch_shapes=[
            *[pltpu.VMEM(*x) for x in shapes],
            pltpu.VMEM((pairs, lane_count, lane_count), jnp.bfloat16),
            pltpu.VMEM((pairs, group_count + 1, pno_count, block_count * lane_count), jnp.bfloat16),
            pltpu.VMEM((pairs, pno_count, lane_count), jnp.float32),
            *project_scratch(bases, pieces),
        ],
        compiler_params=pltpu.CompilerParams(vmem_limit_bytes=24 * 2**20),
        cost_estimate=pl.CostEstimate(
            flops=project_flops(bases, pieces) + 6 * products, bytes_accessed=2**20, transcendentals=0
        ),
    )(*operands)


def gather_pieces(mine, axis):
    count = lax.axis_size(axis)
    up, down = [mine], []
    for shift in range(1, count):
        if shift <= count // 2:
            up.append(from_behind(up[-1], axis, 1))
        else:
            down.append(from_behind(down[-1] if down else mine, axis, count - 1))
    return up + down[::-1]


def on_device_shared(pno_basis, amplitudes, send_list, couple, couple_weight, fit_weight, fit_blocks):
    pair_count, pno_count, _ = pno_basis.shape
    group_total = lax.axis_size("blk")
    pieces = gather_pieces(fit_blocks, "dom")
    across = from_partner(pno_basis, "blk", 2)
    far = [([from_behind(fit_blocks, "blk", by)], by) for by in range(SET, group_total, SET)]
    pair_amps = amplitudes.reshape(pair_count, pno_count, pno_count)
    sent = pack_pairs(send_list.reshape(-1), pno_basis, pair_amps)
    sent, *heads = lax.optimization_barrier((sent, *[group[0] for group, _ in far]))
    far = [([head], by) for head, (_, by) in zip(heads, far)]
    coupled = lax.all_to_all(sent, "blk", split_axis=0, concat_axis=0, tiled=True)
    across, pieces[1], pieces[-1] = lax.optimization_barrier((across, pieces[1], pieces[-1]))
    bases = [pno_basis, from_partner(pno_basis, "blk", 1), across, from_partner(across, "blk", 1)]
    coupled, *bases = lax.optimization_barrier((coupled, *bases))
    own, updated = dress(couple, couple_weight, fit_weight, pno_basis, pair_amps, coupled)
    last = len(pieces) // 2
    _, pieces[last] = lax.optimization_barrier((own, pieces[last]))
    groups = [pieces]
    for group, by in far:
        group += [from_behind(x, "blk", by) for x in pieces[1:]]
        if last > 1:
            source, pieces[last] = lax.optimization_barrier((group[0], pieces[last]))
            group[-1] = from_behind(source, "dom", len(pieces) - 1)
        groups.append(group)
    inner = [project(bases, group) for group in groups[:-1]]
    final = groups[-1]
    dressed = [own, *[from_partner(own, "blk", flip) for flip in range(1, SET)]]
    for members in ((2, 3), (0, 1)):
        partial = finish(
            members, inner, [bases[member] for member in members], final, [dressed[member] for member in members]
        )
        if members[0]:
            partial, *final = lax.optimization_barrier((partial, *final))
            for member, x in zip(members, partial):
                updated = updated + from_partner(x, "blk", member)
        else:
            mine, beside = partial
            updated, mine, beside = lax.optimization_barrier((updated, mine, from_partner(beside, "blk", 1)))
            updated = updated + mine + beside
    return updated.reshape(pair_count, pno_count * pno_count)


def dress_with(pair_amps, intersection, partner_amps, weights):
    half_product = jnp.einsum("pcab,pcbe->pcae", intersection, partner_amps, precision=HIGHEST)
    sandwich = jnp.einsum("pcae,pcfe->pcaf", half_product, intersection, precision=HIGHEST)
    return pair_amps + jnp.einsum("pc,pcaf->paf", weights, sandwich, precision=HIGHEST)


def fit_term(pair_basis, dressed, blocks, weights):
    pair_count, pno_count, orbital_count = pair_basis.shape
    flat_basis = pair_basis.reshape(pair_count * pno_count, orbital_count)
    stacked = blocks.reshape(2 * orbital_count, orbital_count)
    projected = jnp.dot(
        flat_basis, stacked.T, precision=HIGHEST, preferred_element_type=jnp.float32
    )
    projected = projected.reshape(pair_count, pno_count, 2, orbital_count)
    inner_blocks = jnp.einsum("par,pbmr->mpab", pair_basis, projected, precision=HIGHEST)
    left_product = jnp.einsum("pai,pij->paj", inner_blocks[0], dressed, precision=HIGHEST)
    fit_contrib = jnp.einsum("paj,pbj->pab", left_product, inner_blocks[1], precision=HIGHEST)
    return weights[:, None, None] * fit_contrib


def on_device_ring(pno_basis, amplitudes, send_list, couple, couple_weight, fit_weight, fit_blocks):
    pair_count, pno_count, _ = pno_basis.shape
    block_count = fit_blocks.shape[0]
    pair_amps = amplitudes.reshape(pair_count, pno_count, pno_count)
    send_order = send_list.reshape(-1)
    basis_in = lax.all_to_all(jnp.take(pno_basis, send_order, axis=0), "blk", split_axis=0, concat_axis=0, tiled=True)
    amps_in = lax.all_to_all(jnp.take(pair_amps, send_order, axis=0), "blk", split_axis=0, concat_axis=0, tiled=True)
    partner_basis = jnp.take(basis_in, couple, axis=0)
    intersection = jnp.einsum("par,pcbr->pcab", pno_basis, partner_basis, precision=HIGHEST)
    dressed = dress_with(pair_amps, intersection, jnp.take(amps_in, couple, axis=0), couple_weight)
    updated = dressed
    current = lax.all_gather(fit_blocks, "dom", axis=2, tiled=True)
    for stop in range(fit_weight.shape[1] // block_count):
        if stop > 0:
            current = from_behind(current, "blk", 1)
        for b in range(block_count):
            updated = updated + fit_term(pno_basis, dressed, current[b], fit_weight[:, stop * block_count + b])
    return updated.reshape(pair_count, pno_count * pno_count)


def solution(mesh):
    placed = (
        P(("blk", "dom"), None, None),
        P(("blk", "dom"), None),
        P("blk", "dom", None, None),
        P(("blk", "dom"), None),
        P(("blk", "dom"), None),
        P(("blk", "dom"), None),
        P("blk", None, "dom", None),
    )

    def on_device(*args):
        send_list, fit_weight, fit_blocks = args[2], args[5], args[6]
        group_total = mesh.shape["blk"]
        meets_all = fit_weight.shape[1] == group_total * fit_blocks.shape[0]
        if meets_all and group_total % SET == 0 and group_total > SET and group_total & (group_total - 1) == 0 and send_list.shape[3] == 1:
            return on_device_shared(*args)
        return on_device_ring(*args)

    return jax.shard_map(
        on_device, mesh=mesh, in_specs=placed, out_specs=P(("blk", "dom"), None), check_vma=False
    )
```

profile of v0, /device:TPU:0, one launch (start us, length us, event | category | flops | bytes accessed | tf_op | source)
XLA Modules:
  0.0 55.3 jit_solution(17271190513158244544)
XLA Ops:
  0.0 3.0 %collective-permute-start.2 = (f32[8,64,256]{2,1,0:T(8,128)}, f32[8,64,256]{2,1,0:T(8,128)S(1)}, u32[]{:S(2)}, u32[]{:S(2)}) collective-permute-start(f32[8,64,256]{2,1,0:T(8,128)} %refs_2_), channel_id=1, source_target_pairs={{0,8},{4,12},{8,0},{12,4},{16,24},{20,28},{24,16},{28,20},{1,9},{5... | collective-permute-start | bytes 1572872 | tf_op jit(solution)/shard_map/ppermute | solution.py:33
  3.0 1.5 %collective-permute-start = (f32[2,2,64,256]{3,2,1,0:T(8,128)}, f32[2,2,64,256]{3,2,1,0:T(8,128)S(1)}, u32[]{:S(2)}, u32[]{:S(2)}) collective-permute-start(f32[2,2,64,256]{3,2,1,0:T(8,128)} %refs_4_.1), channel_id=1, source_target_pairs={{0,16},{4,20},{8,24},{12,28},{16,0},{20,4},{24,8},{28,12},{1,17},{... | collective-permute-start | bytes 786440 | tf_op jit(solution)/shard_map/ppermute | solution.py:38
  4.5 1.6 %collective-permute-start.3 = (f32[2,2,64,256]{3,2,1,0:T(8,128)}, f32[2,2,64,256]{3,2,1,0:T(8,128)S(1)}, u32[]{:S(2)}, u32[]{:S(2)}) collective-permute-start(f32[2,2,64,256]{3,2,1,0:T(8,128)} %refs_4_.1), channel_id=1, source_target_pairs={{0,1},{1,2},{2,3},{3,0},{4,5},{5,6},{6,7},{7,4},{8,9},{9,10},{10,1... | collective-permute-start | bytes 786440 | tf_op jit(solution)/shard_map/ppermute | solution.py:38
  6.1 2.2 %collective-permute-start.4 = (f32[2,2,64,256]{3,2,1,0:T(8,128)}, f32[2,2,64,256]{3,2,1,0:T(8,128)S(1)}, u32[]{:S(2)}, u32[]{:S(2)}) collective-permute-start(f32[2,2,64,256]{3,2,1,0:T(8,128)} %refs_4_.1), channel_id=1, source_target_pairs={{0,3},{1,0},{2,1},{3,2},{4,7},{5,4},{6,5},{7,6},{8,11},{9,8},{10,9... | collective-permute-start | bytes 786440 | tf_op jit(solution)/shard_map/ppermute | solution.py:38
  8.4 1.0 %reshape.9.amps = f32[8,64,64]{2,1,0:T(8,128)S(1)} reshape(f32[8,4096]{1,0:T(8,128)} %param.8) | data formatting | bytes 262144 | tf_op jit(solution)/shard_map/reshape | solution.py:333
  9.4 0.0 copy-start
  9.4 1.0 %copy-done = f32[8,64,256]{2,1,0:T(8,128)S(1)} copy-done((f32[8,64,256]{2,1,0:T(8,128)S(1)}, f32[8,64,256]{2,1,0:T(8,128)}, u32[]{:S(2)}) %copy-start) | copy-done | bytes 524312
  10.4 0.7 %copy-done.2 = s32[1,1,8,1]{2,3,1,0:T(1,128)S(1)} copy-done((s32[1,1,8,1]{2,3,1,0:T(1,128)S(1)}, s32[1,1,8,1]{2,3,1,0:T(1,128)}, u32[]{:S(2)}) %copy-start.2) | copy-done | bytes 56
  11.1 1.5 %shard_map.73 = f32[8,80,256]{2,1,0:T(8,128)} custom-call(s32[8]{0:T(128)S(1)} %bitcast.6, f32[8,64,256]{2,1,0:T(8,128)S(1)} %copy-done, f32[8,64,64]{2,1,0:T(8,128)S(1)} %reshape.9.amps), custom_call_target="tpu_custom_call" | custom-call | bytes 524288 | tf_op jit(solution)/shard_map/pallas_call | solution.py:59
  12.6 0.0 collective-permute-done.refs_4_
  12.6 3.5 %all-to-all-start = ((f32[8,80,256]{2,1,0:T(8,128)}), f32[8,80,256]{2,1,0:T(8,128)S(1)}, u32[]{:S(2)}, u32[]{:S(2)}) async-start(f32[8,80,256]{2,1,0:T(8,128)} %shard_map.73), calls=%async_computation | async-start | bytes 1310720 | tf_op jit(solution)/shard_map/all_to_all | solution.py:337
  16.1 0.0 copy-done.1
  16.1 0.0 copy-start.3
  16.1 0.4 collective-permute-start.1
  16.6 0.0 collective-permute-done.3.refs_5_
  16.6 2.6 %collective-permute-done.4.refs_7_ = f32[2,2,64,256]{3,2,1,0:T(8,128)S(1)} collective-permute-done((f32[2,2,64,256]{3,2,1,0:T(8,128)}, f32[2,2,64,256]{3,2,1,0:T(8,128)S(1)}, u32[]{:S(2)}, u32[]{:S(2)}) %collective-permute-start.4) | collective-permute-done | bytes 262176 | tf_op jit(solution)/shard_map/ppermute | solution.py:38
  19.1 0.7 %copy-done.6 = f32[2,2,64,256]{3,2,1,0:T(8,128)} copy-done((f32[2,2,64,256]{3,2,1,0:T(8,128)}, f32[2,2,64,256]{3,2,1,0:T(8,128)S(1)}, u32[]{:S(2)}) %copy-start.6) | copy-done | bytes 262168
  19.9 0.0 collective-permute-done.2.refs_2_
  19.9 0.0 collective-permute-start.5
  19.9 1.2 %collective-permute-start.6 = (f32[2,2,64,256]{3,2,1,0:T(8,128)}, f32[2,2,64,256]{3,2,1,0:T(8,128)}, u32[]{:S(2)}, u32[]{:S(2)}) collective-permute-start(f32[2,2,64,256]{3,2,1,0:T(8,128)} %copy-done.4), channel_id=1, source_target_pairs={{0,1},{1,2},{2,3},{3,0},{4,5},{5,6},{6,7},{7,4},{8,9},{9,10},{10,1... | collective-permute-start | bytes 786440 | tf_op jit(solution)/shard_map/ppermute | solution.py:38
  21.0 0.5 collective-permute-start.7
  21.5 0.0 collective-permute-done.1.refs_1_.refs_3_
  21.6 5.8 %all-to-all-done.coupled = f32[8,80,256]{2,1,0:T(8,128)S(1)} async-done(((f32[8,80,256]{2,1,0:T(8,128)}), f32[8,80,256]{2,1,0:T(8,128)S(1)}, u32[]{:S(2)}, u32[]{:S(2)}) %all-to-all-start) | async-done | bytes 655392 | tf_op jit(solution)/shard_map/all_to_all | solution.py:337
  27.3 0.0 collective-permute-done.5.refs_3_
  27.3 0.0 copy-done.8
  27.3 2.2 %shard_map.74 = (f32[8,40,128]{2,1,0:T(8,128)S(1)}, f32[8,32,128]{2,1,0:T(8,128)S(1)}) custom-call(s32[8,8]{1,0:T(8,128)S(1)} %copy-done.8, f32[8,8]{1,0:T(8,128)S(1)} %copy-done.9, f32[8,16]{1,0:T(8,128)S(1)} %copy-done.10, f32[8,64,256]{2,1,0:T(8,128)S(1)} %copy-done.1, f32[8,64,64]{2,1,0:T(8,128)S(1)} %reshape.9.amps, f32[8,80,256]{2,1,0:T(8,128)S(1)} %all-to-all-done.coupled), custom_call_target="tpu_custom_call" | custom-call | flops 4000000000 | bytes 1048576 | tf_op jit(solution)/shard_map/pallas_call | solution.py:101
  29.6 0.6 collective-permute-start.10
  30.1 0.0 collective-permute-start.11
  30.1 0.6 %collective-permute-done.6.refs_6_ = f32[2,2,64,256]{3,2,1,0:T(8,128)} collective-permute-done((f32[2,2,64,256]{3,2,1,0:T(8,128)}, f32[2,2,64,256]{3,2,1,0:T(8,128)}, u32[]{:S(2)}, u32[]{:S(2)}) %collective-permute-start.6) | collective-permute-done | bytes 262176 | tf_op jit(solution)/shard_map/ppermute | solution.py:38
  30.7 0.5 collective-permute-start.8
  31.2 1.4 %collective-permute-start.9 = (f32[2,2,64,256]{3,2,1,0:T(8,128)S(1)}, f32[2,2,64,256]{3,2,1,0:T(8,128)S(1)}, u32[]{:S(2)}, u32[]{:S(2)}) collective-permute-start(f32[2,2,64,256]{3,2,1,0:T(8,128)S(1)} %collective-permute-done.refs_4_), channel_id=1, source_target_pairs={{0,3},{1,0},{2,1},{3,2},{4,7},{5,4},{6,5},{7,6},{8,11},{9,8},{10,9... | collective-permute-start | bytes 786440 | tf_op jit(solution)/shard_map/ppermute | solution.py:38
  32.7 6.8 %shard_map.75 = (bf16[32,128,128]{2,1,0:T(8,128)(2,1)S(1)}, bf16[32,128,256]{2,1,0:T(8,128)(2,1)S(1)}) custom-call(f32[8,64,256]{2,1,0:T(8,128)S(1)} %copy-done.1, f32[8,64,256]{2,1,0:T(8,128)S(1)} %collective-permute-done.1.refs_1_.refs_3_, f32[8,64,256]{2,1,0:T(8,128)S(1)} %collective-permute-done.2.refs_2_, ...), custom_call_target="tpu_custom_call" | custom-call | flops 4026531840 | bytes 1048576 | tf_op jit(solution)/shard_map/pallas_call | solution.py:225
  39.5 0.0 collective-permute-done.7.refs_5_
  39.5 1.2 %collective-permute-start.14 = (f32[8,40,128]{2,1,0:T(8,128)S(1)}, f32[8,40,128]{2,1,0:T(8,128)S(1)}, u32[]{:S(2)}, u32[]{:S(2)}) collective-permute-start(f32[8,40,128]{2,1,0:T(8,128)S(1)} %get-tuple-element.45.refs_8_), channel_id=1, source_target_pairs={{0,4},{4,0},{8,12},{12,8},{16,20},{20,16},{24,28},{28,24},{1,5},{5... | collective-permute-start | bytes 491528 | tf_op jit(solution)/shard_map/ppermute | solution.py:33
  40.7 0.0 collective-permute-done.10.refs_8_
  40.7 0.0 collective-permute-done.11.refs_9_
  40.7 0.0 collective-permute-done.8.refs_6_
  40.7 0.0 collective-permute-done.9.refs_7_
  40.7 5.2 %shard_map.76 = (f32[8,32,128]{2,1,0:T(8,128)S(1)}, f32[8,32,128]{2,1,0:T(8,128)S(1)}) custom-call(bf16[32,128,128]{2,1,0:T(8,128)(2,1)S(1)} %get-tuple-element.49.refs_0_, bf16[32,128,256]{2,1,0:T(8,128)(2,1)S(1)} %get-tuple-element.50.refs_1_, f32[8,64,256]{2,1,0:T(8,128)S(1)} %collective-permute-done.2.refs_2_, ...), custom_call_target="tpu_custom_call" | custom-call | flops 2214592512 | bytes 1048576 | tf_op jit(solution)/shard_map/pallas_call | solution.py:297
  45.8 0.6 %collective-permute-start.13 = (f32[8,32,128]{2,1,0:T(8,128)S(1)}, f32[8,32,128]{2,1,0:T(8,128)S(1)}, u32[]{:S(2)}, u32[]{:S(2)}) collective-permute-start(f32[8,32,128]{2,1,0:T(8,128)S(1)} %get-tuple-element.55), channel_id=1, source_target_pairs={{0,12},{4,8},{8,4},{12,0},{16,28},{20,24},{24,20},{28,16},{1,13},{... | collective-permute-start | bytes 393224 | tf_op jit(solution)/shard_map/ppermute | solution.py:33
  46.5 1.1 %collective-permute-start.12 = (f32[8,32,128]{2,1,0:T(8,128)S(1)}, f32[8,32,128]{2,1,0:T(8,128)S(1)}, u32[]{:S(2)}, u32[]{:S(2)}) collective-permute-start(f32[8,32,128]{2,1,0:T(8,128)S(1)} %get-tuple-element.54), channel_id=1, source_target_pairs={{0,8},{4,12},{8,0},{12,4},{16,24},{20,28},{24,16},{28,20},{1,9},{5... | collective-permute-start | bytes 393224 | tf_op jit(solution)/shard_map/ppermute | solution.py:33
  47.6 0.0 collective-permute-done.14.refs_9_
  47.6 5.2 %shard_map.77 = (f32[8,32,128]{2,1,0:T(8,128)S(1)}, f32[8,32,128]{2,1,0:T(8,128)S(1)}) custom-call(bf16[32,128,128]{2,1,0:T(8,128)(2,1)S(1)} %get-tuple-element.49.refs_0_, bf16[32,128,256]{2,1,0:T(8,128)(2,1)S(1)} %get-tuple-element.50.refs_1_, f32[8,64,256]{2,1,0:T(8,128)S(1)} %copy-done.1, f32[8,64,256]{2,1,0:T(8,128)S(1)} %collective-permute-done.1.refs_1_.refs_3_, ...), custom_call_target="tpu_custom_call" | custom-call | flops 2214592512 | bytes 1048576 | tf_op jit(solution)/shard_map/pallas_call | solution.py:297
  52.7 0.3 collective-permute-start.15
  53.0 0.0 collective-permute-done.13
  53.0 1.5 %collective-permute-done.12 = f32[8,32,128]{2,1,0:T(8,128)S(1)} collective-permute-done((f32[8,32,128]{2,1,0:T(8,128)S(1)}, f32[8,32,128]{2,1,0:T(8,128)S(1)}, u32[]{:S(2)}, u32[]{:S(2)}) %collective-permute-start.12) | collective-permute-done | bytes 131104 | tf_op jit(solution)/shard_map/ppermute | solution.py:33
  54.6 0.0 collective-permute-done.15
  54.6 0.7 %copy.10 = f32[1,8,32,128]{3,1,2,0:T(8,128)} copy(f32[1,8,32,128]{3,2,1,0:T(8,128)S(1)} %add_bitcast_fusion) | data formatting | bytes 262144
  (17 shorter events, 0.1 us)
Async XLA Ops:
  0.0 27.3 %copy-start.8 = (s32[8,8]{1,0:T(8,128)S(1)}, s32[8,8]{1,0:T(8,128)}, u32[]{:S(2)}) copy-start(s32[8,8]{1,0:T(8,128)} %couple.1) | copy-start | bytes 772
  0.0 27.3 %copy-start.9 = (f32[8,8]{1,0:T(8,128)S(1)}, f32[8,8]{1,0:T(8,128)}, u32[]{:S(2)}) copy-start(f32[8,8]{1,0:T(8,128)} %couple_weight.1) | copy-start | bytes 772
  0.0 27.3 %copy-start.10 = (f32[8,16]{1,0:T(8,128)S(1)}, f32[8,16]{1,0:T(8,128)}, u32[]{:S(2)}) copy-start(f32[8,16]{1,0:T(8,128)} %fit_weight.1) | copy-start | bytes 1540
  0.0 19.9 %collective-permute-start.2 = (f32[8,64,256]{2,1,0:T(8,128)}, f32[8,64,256]{2,1,0:T(8,128)S(1)}, u32[]{:S(2)}, u32[]{:S(2)}) collective-permute-start(f32[8,64,256]{2,1,0:T(8,128)} %refs_2_), channel_id=1, source_target_pairs={{0,8},{4,12},{8,0},{12,4},{16,24},{20,28},{24,16},{28,20},{1,9},{5... | collective-permute-start | bytes 1572872 | tf_op jit(solution)/shard_map/ppermute | solution.py:33
  3.0 9.6 %collective-permute-start = (f32[2,2,64,256]{3,2,1,0:T(8,128)}, f32[2,2,64,256]{3,2,1,0:T(8,128)S(1)}, u32[]{:S(2)}, u32[]{:S(2)}) collective-permute-start(f32[2,2,64,256]{3,2,1,0:T(8,128)} %refs_4_.1), channel_id=1, source_target_pairs={{0,16},{4,20},{8,24},{12,28},{16,0},{20,4},{24,8},{28,12},{1,17},{... | collective-permute-start | bytes 786440 | tf_op jit(solution)/shard_map/ppermute | solution.py:38
  4.5 12.1 %collective-permute-start.3 = (f32[2,2,64,256]{3,2,1,0:T(8,128)}, f32[2,2,64,256]{3,2,1,0:T(8,128)S(1)}, u32[]{:S(2)}, u32[]{:S(2)}) collective-permute-start(f32[2,2,64,256]{3,2,1,0:T(8,128)} %refs_4_.1), channel_id=1, source_target_pairs={{0,1},{1,2},{2,3},{3,0},{4,5},{5,6},{6,7},{7,4},{8,9},{9,10},{10,1... | collective-permute-start | bytes 786440 | tf_op jit(solution)/shard_map/ppermute | solution.py:38
  6.1 13.0 %collective-permute-start.4 = (f32[2,2,64,256]{3,2,1,0:T(8,128)}, f32[2,2,64,256]{3,2,1,0:T(8,128)S(1)}, u32[]{:S(2)}, u32[]{:S(2)}) collective-permute-start(f32[2,2,64,256]{3,2,1,0:T(8,128)} %refs_4_.1), channel_id=1, source_target_pairs={{0,3},{1,0},{2,1},{3,2},{4,7},{5,4},{6,5},{7,6},{8,11},{9,8},{10,9... | collective-permute-start | bytes 786440 | tf_op jit(solution)/shard_map/ppermute | solution.py:38
  9.4 1.0 %copy-start = (f32[8,64,256]{2,1,0:T(8,128)S(1)}, f32[8,64,256]{2,1,0:T(8,128)}, u32[]{:S(2)}) copy-start(f32[8,64,256]{2,1,0:T(8,128)} %refs_2_) | copy-start | bytes 1572868
  10.4 0.7 %copy-start.2 = (s32[1,1,8,1]{2,3,1,0:T(1,128)S(1)}, s32[1,1,8,1]{2,3,1,0:T(1,128)}, u32[]{:S(2)}) copy-start(s32[1,1,8,1]{2,3,1,0:T(1,128)} %param.9) | copy-start | bytes 100
  11.1 5.1 %copy-start.1 = (f32[8,64,256]{2,1,0:T(8,128)S(1)}, f32[8,64,256]{2,1,0:T(8,128)}, u32[]{:S(2)}) copy-start(f32[8,64,256]{2,1,0:T(8,128)} %refs_2_) | copy-start | bytes 1572868
  12.6 14.7 %all-to-all-start = ((f32[8,80,256]{2,1,0:T(8,128)}), f32[8,80,256]{2,1,0:T(8,128)S(1)}, u32[]{:S(2)}, u32[]{:S(2)}) async-start(f32[8,80,256]{2,1,0:T(8,128)} %shard_map.73), calls=%async_computation | async-start | bytes 1310720 | tf_op jit(solution)/shard_map/all_to_all | solution.py:337
  16.1 16.5 %copy-start.3 = (f32[2,2,64,256]{3,2,1,0:T(8,128)S(1)}, f32[2,2,64,256]{3,2,1,0:T(8,128)}, u32[]{:S(2)}) copy-start(f32[2,2,64,256]{3,2,1,0:T(8,128)} %refs_4_.1) | copy-start | bytes 786436
  16.1 5.4 %collective-permute-start.1 = (f32[8,64,256]{2,1,0:T(8,128)S(1)}, f32[8,64,256]{2,1,0:T(8,128)S(1)}, u32[]{:S(2)}, u32[]{:S(2)}) collective-permute-start(f32[8,64,256]{2,1,0:T(8,128)S(1)} %copy-done.1), channel_id=1, source_target_pairs={{0,4},{4,0},{8,12},{12,8},{16,20},{20,16},{24,28},{28,24},{1,5},{5... | collective-permute-start | bytes 1572872 | tf_op jit(solution)/shard_map/ppermute | solution.py:33
  16.6 2.6 %copy-start.4 = (f32[2,2,64,256]{3,2,1,0:T(8,128)}, f32[2,2,64,256]{3,2,1,0:T(8,128)S(1)}, u32[]{:S(2)}) copy-start(f32[2,2,64,256]{3,2,1,0:T(8,128)S(1)} %collective-permute-done.3.refs_5_) | copy-start | bytes 786436
  19.1 0.7 %copy-start.6 = (f32[2,2,64,256]{3,2,1,0:T(8,128)}, f32[2,2,64,256]{3,2,1,0:T(8,128)S(1)}, u32[]{:S(2)}) copy-start(f32[2,2,64,256]{3,2,1,0:T(8,128)S(1)} %collective-permute-done.4.refs_7_) | copy-start | bytes 786436
  19.9 7.4 %collective-permute-start.5 = (f32[8,64,256]{2,1,0:T(8,128)S(1)}, f32[8,64,256]{2,1,0:T(8,128)S(1)}, u32[]{:S(2)}, u32[]{:S(2)}) collective-permute-start(f32[8,64,256]{2,1,0:T(8,128)S(1)} %collective-permute-done.2.refs_2_), channel_id=1, source_target_pairs={{0,4},{4,0},{8,12},{12,8},{16,20},{20,16},{24,28},{28,24},{1,5},{5... | collective-permute-start | bytes 1572872 | tf_op jit(solution)/shard_map/ppermute | solution.py:33
  19.9 10.8 %collective-permute-start.6 = (f32[2,2,64,256]{3,2,1,0:T(8,128)}, f32[2,2,64,256]{3,2,1,0:T(8,128)}, u32[]{:S(2)}, u32[]{:S(2)}) collective-permute-start(f32[2,2,64,256]{3,2,1,0:T(8,128)} %copy-done.4), channel_id=1, source_target_pairs={{0,1},{1,2},{2,3},{3,0},{4,5},{5,6},{6,7},{7,4},{8,9},{9,10},{10,1... | collective-permute-start | bytes 786440 | tf_op jit(solution)/shard_map/ppermute | solution.py:38
  21.0 18.4 %collective-permute-start.7 = (f32[2,2,64,256]{3,2,1,0:T(8,128)}, f32[2,2,64,256]{3,2,1,0:T(8,128)}, u32[]{:S(2)}, u32[]{:S(2)}) collective-permute-start(f32[2,2,64,256]{3,2,1,0:T(8,128)} %copy-done.4), channel_id=1, source_target_pairs={{0,16},{4,20},{8,24},{12,28},{16,0},{20,4},{24,8},{28,12},{1,17},{... | collective-permute-start | bytes 786440 | tf_op jit(solution)/shard_map/ppermute | solution.py:38
  27.3 5.3 %copy-start.5 = (f32[2,2,64,256]{3,2,1,0:T(8,128)S(1)}, f32[2,2,64,256]{3,2,1,0:T(8,128)}, u32[]{:S(2)}) copy-start(f32[2,2,64,256]{3,2,1,0:T(8,128)} %copy-done.4) | copy-start | bytes 786436
  27.3 5.3 %copy-start.7 = (f32[2,2,64,256]{3,2,1,0:T(8,128)S(1)}, f32[2,2,64,256]{3,2,1,0:T(8,128)}, u32[]{:S(2)}) copy-start(f32[2,2,64,256]{3,2,1,0:T(8,128)} %copy-done.6) | copy-start | bytes 786436
  29.6 11.1 %collective-permute-start.10 = (f32[8,40,128]{2,1,0:T(8,128)S(1)}, f32[8,40,128]{2,1,0:T(8,128)S(1)}, u32[]{:S(2)}, u32[]{:S(2)}) collective-permute-start(f32[8,40,128]{2,1,0:T(8,128)S(1)} %get-tuple-element.45.refs_8_), channel_id=1, source_target_pairs={{0,8},{4,12},{8,0},{12,4},{16,24},{20,28},{24,16},{28,20},{1,9},{5... | collective-permute-start | bytes 491528 | tf_op jit(solution)/shard_map/ppermute | solution.py:33
  30.1 10.6 %collective-permute-start.11 = (f32[8,40,128]{2,1,0:T(8,128)S(1)}, f32[8,40,128]{2,1,0:T(8,128)S(1)}, u32[]{:S(2)}, u32[]{:S(2)}) collective-permute-start(f32[8,40,128]{2,1,0:T(8,128)S(1)} %get-tuple-element.45.refs_8_), channel_id=1, source_target_pairs={{0,12},{4,8},{8,4},{12,0},{16,28},{20,24},{24,20},{28,16},{1,13},{... | collective-permute-start | bytes 491528 | tf_op jit(solution)/shard_map/ppermute | solution.py:33
  30.7 10.0 %collective-permute-start.8 = (f32[2,2,64,256]{3,2,1,0:T(8,128)}, f32[2,2,64,256]{3,2,1,0:T(8,128)S(1)}, u32[]{:S(2)}, u32[]{:S(2)}) collective-permute-start(f32[2,2,64,256]{3,2,1,0:T(8,128)} %collective-permute-done.6.refs_6_), channel_id=1, source_target_pairs={{0,16},{4,20},{8,24},{12,28},{16,0},{20,4},{24,8},{28,12},{1,17},{... | collective-permute-start | bytes 786440 | tf_op jit(solution)/shard_map/ppermute | solution.py:38
  31.2 9.5 %collective-permute-start.9 = (f32[2,2,64,256]{3,2,1,0:T(8,128)S(1)}, f32[2,2,64,256]{3,2,1,0:T(8,128)S(1)}, u32[]{:S(2)}, u32[]{:S(2)}) collective-permute-start(f32[2,2,64,256]{3,2,1,0:T(8,128)S(1)} %collective-permute-done.refs_4_), channel_id=1, source_target_pairs={{0,3},{1,0},{2,1},{3,2},{4,7},{5,4},{6,5},{7,6},{8,11},{9,8},{10,9... | collective-permute-start | bytes 786440 | tf_op jit(solution)/shard_map/ppermute | solution.py:38
  39.5 8.1 %collective-permute-start.14 = (f32[8,40,128]{2,1,0:T(8,128)S(1)}, f32[8,40,128]{2,1,0:T(8,128)S(1)}, u32[]{:S(2)}, u32[]{:S(2)}) collective-permute-start(f32[8,40,128]{2,1,0:T(8,128)S(1)} %get-tuple-element.45.refs_8_), channel_id=1, source_target_pairs={{0,4},{4,0},{8,12},{12,8},{16,20},{20,16},{24,28},{28,24},{1,5},{5... | collective-permute-start | bytes 491528 | tf_op jit(solution)/shard_map/ppermute | solution.py:33
  45.8 7.2 %collective-permute-start.13 = (f32[8,32,128]{2,1,0:T(8,128)S(1)}, f32[8,32,128]{2,1,0:T(8,128)S(1)}, u32[]{:S(2)}, u32[]{:S(2)}) collective-permute-start(f32[8,32,128]{2,1,0:T(8,128)S(1)} %get-tuple-element.55), channel_id=1, source_target_pairs={{0,12},{4,8},{8,4},{12,0},{16,28},{20,24},{24,20},{28,16},{1,13},{... | collective-permute-start | bytes 393224 | tf_op jit(solution)/shard_map/ppermute | solution.py:33
  46.5 8.0 %collective-permute-start.12 = (f32[8,32,128]{2,1,0:T(8,128)S(1)}, f32[8,32,128]{2,1,0:T(8,128)S(1)}, u32[]{:S(2)}, u32[]{:S(2)}) collective-permute-start(f32[8,32,128]{2,1,0:T(8,128)S(1)} %get-tuple-element.54), channel_id=1, source_target_pairs={{0,8},{4,12},{8,0},{12,4},{16,24},{20,28},{24,16},{28,20},{1,9},{5... | collective-permute-start | bytes 393224 | tf_op jit(solution)/shard_map/ppermute | solution.py:33
  52.7 1.8 %collective-permute-start.15 = (f32[8,32,128]{2,1,0:T(8,128)S(1)}, f32[8,32,128]{2,1,0:T(8,128)S(1)}, u32[]{:S(2)}, u32[]{:S(2)}) collective-permute-start(f32[8,32,128]{2,1,0:T(8,128)S(1)} %get-tuple-element.61), channel_id=1, source_target_pairs={{0,4},{4,0},{8,12},{12,8},{16,20},{20,16},{24,28},{28,24},{1,5},{5... | collective-permute-start | bytes 393224 | tf_op jit(solution)/shard_map/ppermute | solution.py:33
where the time goes:
time: 55.7 us; the launch traced here: 55.3 us
  Pallas kernels  20.8 us (37%)
  starting transfers between devices  19.7 us (35%)
  waiting for transfers between devices  10.4 us (19%)
  local copies, waits for them, and re-layouts  4.18 us (8%)
    pallas_call x2, Pallas kernels, finish(): pl.pallas_call(lambda *refs: finish_kernel(members, group_count, len(piec...  10.3 us
    ppermute x7, starting transfers between devices, from_behind(): return lax.ppermute(x, axis, [(i, (i + by) % count) for i in range(count)])  8.97 us
    ppermute x9, starting transfers between devices, from_partner(): lax.ppermute(x, axis, [(i, i ^ flip) for i in range(lax.axis_size(axis))])  7.17 us
    pallas_call x1, Pallas kernels, project(): pl.pallas_call(lambda *refs: project_kernel(len(bases), *refs), out_shape...  6.81 us
    all_to_all x1, waiting for transfers between devices, on_device_shared(): lax.all_to_all(sent, 'blk', split_axis=0, concat_axis=0, tiled=True)  5.75 us
    all_to_all x1, starting transfers between devices, on_device_shared(): lax.all_to_all(sent, 'blk', split_axis=0, concat_axis=0, tiled=True)  3.54 us
    unnamed x23, local copies, waits for them, and re-layouts  3.17 us
    ppermute x7, waiting for transfers between devices, from_behind(): return lax.ppermute(x, axis, [(i, (i + by) % count) for i in range(count)])  3.16 us
  transfers between devices with their start and end apart: 17, of which 4 were waited for; matrix products, arithmetic and copies ran while one was open for 2% of the time, Pallas kernels for 38%

commit v1 on v0

--- a/solution.py
+++ b/solution.py
@@ -42,34 +42,54 @@
     return [pl.BlockSpec(memory_space=pltpu.VMEM)] * count
 
 
-def pack_kernel(send, basis, amps, out):
-    pno_count = amps.shape[1]
-    lanes = basis.shape[2] // pno_count
-    step = pno_count // lanes
-    for peer in range(out.shape[0]):
-        pair = send[peer]
-        out[peer, :pno_count] = basis[pair]
-        listed = amps[pair]
-        out[peer, pno_count:] = stack([listed[i * step:(i + 1) * step] for i in range(lanes)], 1)
+def pack_kernel(send, basis, amps, out, rows, sent):
+    peer_count, row_count, lane_count = rows.shape
+    pno_count = out.shape[1] - row_count
+    copies = []
+    for peer in range(peer_count):
+        copies.append(pltpu.make_async_copy(basis.at[send[peer]], out.at[peer, pl.ds(0, pno_count)], sent.at[0, peer]))
+        copies[-1].start()
+    for peer in range(peer_count):
+        for i in range(row_count):
+            rows[peer, i:i + 1, :] = amps[pl.ds(send[peer], 1), i * lane_count:(i + 1) * lane_count]
+        copies.append(pltpu.make_async_copy(rows.at[peer], out.at[peer, pl.ds(pno_count, row_count)], sent.at[1, peer]))
+        copies[-1].start()
+    for copy in copies:
+        copy.wait()
 
 
 def pack_pairs(send_order, basis, amps):
     _, pno_count, orbital_count = basis.shape
-    rows = pno_count + pno_count * pno_count // orbital_count
+    peer_count, rows = send_order.shape[0], amps.shape[1] // orbital_count
     return pl.pallas_call(
         pack_kernel,
-        out_shape=jax.ShapeDtypeStruct((send_order.shape[0], rows, orbital_count), jnp.float32),
-        in_specs=[pl.BlockSpec(memory_space=pltpu.SMEM), *vmem(2)],
-        out_specs=vmem(1)[0],
+        out_shape=jax.ShapeDtypeStruct((peer_count, pno_count + rows, orbital_count), jnp.float32),
+        in_specs=[
+            pl.BlockSpec(memory_space=pltpu.SMEM),
+            pl.BlockSpec(memory_space=pl.ANY),
+            *vmem(1),
+        ],
+        out_specs=pl.BlockSpec(memory_space=pl.ANY),
+        scratch_shapes=[
+            pltpu.VMEM((peer_count, rows, orbital_count), jnp.float32),
+            pltpu.SemaphoreType.DMA((2, peer_count)),
+        ],
         compiler_params=pltpu.CompilerParams(vmem_limit_bytes=4 * 2**20),
         cost_estimate=pl.CostEstimate(flops=0, bytes_accessed=4 * basis.size, transcendentals=0),
     )(send_order, basis, amps)
 
 
-def dress_kernel(couple, couple_weight, fit_weight, basis, amps, coupled, dressed, result, turned):
+def dress_kernel(couple, couple_weight, fit_weight, basis, amps, coupled, dressed, result, turned, paired, partners):
     pair_count, pno_count, orbital_count = basis.shape
     half = pno_count // 2
     slot_count = coupled.shape[0]
+    width = 2 * pno_count
+    for i in range(half):
+        paired[pl.ds(i, pair_count, stride=half), :] = amps[:, i * width:(i + 1) * width]
+    for pair in range(pair_count):
+        packed = paired[pair * half:(pair + 1) * half]
+        for i in range(2):
+            turned[pair, pl.ds(i, half, stride=2), :] = packed[:, i * pno_count:(i + 1) * pno_count]
     own = halves(basis[...].reshape(pair_count * pno_count, orbital_count))
     others = halves(coupled[:, :pno_count].reshape(slot_count * pno_count, orbital_count))
     overlap = halves(dot3(own, others, NT))
@@ -77,15 +97,18 @@
     for slot in range(slot_count):
         cols = slice(slot * pno_count, (slot + 1) * pno_count)
         packed = coupled[slot, pno_count:]
-        partner = stack([packed[:, i:i + pno_count] for i in range(0, orbital_count, pno_count)])
-        left.append(dot3([x[:, cols] for x in overlap], halves(partner), NN))
+        step = orbital_count // pno_count
+        for i in range(step):
+            lanes = slice(i * pno_count, (i + 1) * pno_count)
+            partners[slot, pl.ds(i, packed.shape[0], stride=step), :] = packed[:, lanes]
+        left.append(dot3([x[:, cols] for x in overlap], halves(partners[slot]), NN))
         named = jnp.where(couple[...] == slot, couple_weight[...], 0.0)
         slot_weight.append(jnp.sum(named, axis=1, keepdims=True))
     dressed[:, half:, :] = jnp.zeros((pair_count, dressed.shape[1] - half, 2 * pno_count), jnp.float32)
     for pair in range(pair_count):
         rows = slice(pair * pno_count, (pair + 1) * pno_count)
         scaled = stack([x[rows] * w[pair:pair + 1] for x, w in zip(left, slot_weight)], 1)
-        total = amps[pair] + dot3(halves(scaled), [x[rows] for x in overlap], NT)
+        total = turned[pair] + dot3(halves(scaled), [x[rows] for x in overlap], NT)
         dressed[pair, :half] = stack([total[:half], total[half:]], 1)
         turned[pair] = total
         result[pair] = two_to_one(turned, pair, half)
@@ -105,7 +128,11 @@
         ),
         in_specs=vmem(6),
         out_specs=tuple(vmem(2)),
-        scratch_shapes=[pltpu.VMEM((pair_count, pno_count, pno_count), jnp.float32)],
+        scratch_shapes=[
+            pltpu.VMEM((pair_count, pno_count, pno_count), jnp.float32),
+            pltpu.VMEM((pair_count * pno_count // 2, 2 * pno_count), jnp.float32),
+            pltpu.VMEM((coupled.shape[0], pno_count, pno_count), jnp.float32),
+        ],
         compiler_params=pltpu.CompilerParams(vmem_limit_bytes=10 * 2**20),
         cost_estimate=pl.CostEstimate(flops=4 * 10**9, bytes_accessed=8 * basis.size, transcendentals=0),
     )(couple, couple_weight, fit_weight, basis, amps, coupled)
@@ -330,22 +357,21 @@
     pieces = gather_pieces(fit_blocks, "dom")
     across = from_partner(pno_basis, "blk", 2)
     far = [([from_behind(fit_blocks, "blk", by)], by) for by in range(SET, group_total, SET)]
-    pair_amps = amplitudes.reshape(pair_count, pno_count, pno_count)
-    sent = pack_pairs(send_list.reshape(-1), pno_basis, pair_amps)
+    sent = pack_pairs(send_list.reshape(-1), pno_basis, amplitudes)
     sent, *heads = lax.optimization_barrier((sent, *[group[0] for group, _ in far]))
     far = [([head], by) for head, (_, by) in zip(heads, far)]
     coupled = lax.all_to_all(sent, "blk", split_axis=0, concat_axis=0, tiled=True)
     across, pieces[1], pieces[-1] = lax.optimization_barrier((across, pieces[1], pieces[-1]))
     bases = [pno_basis, from_partner(pno_basis, "blk", 1), across, from_partner(across, "blk", 1)]
     coupled, *bases = lax.optimization_barrier((coupled, *bases))
-    own, updated = dress(couple, couple_weight, fit_weight, pno_basis, pair_amps, coupled)
+    own, updated = dress(couple, couple_weight, fit_weight, pno_basis, amplitudes, coupled)
     last = len(pieces) // 2
     _, pieces[last] = lax.optimization_barrier((own, pieces[last]))
     groups = [pieces]
     for group, by in far:
         group += [from_behind(x, "blk", by) for x in pieces[1:]]
         if last > 1:
-            source, pieces[last] = lax.optimization_barrier((group[0], pieces[last]))
+            source, pieces[-1] = lax.optimization_barrier((group[0], pieces[-1]))
             group[-1] = from_behind(source, "dom", len(pieces) - 1)
         groups.append(group)
     inner = [project(bases, group) for group in groups[:-1]]

time: 55.7 us -> 55.2 us (level)
  waiting for transfers between devices: 10.4 us -> 9.09 us
    all_to_all x1, waiting for transfers between devices: 5.75 us -> 3.08 us  [on_device_shared(): lax.all_to_all(sent, 'blk', split_axis=0, concat_axis=0, tiled=True)]
    ppermute x7, waiting for transfers between devices: 3.16 us -> 4.75 us  [from_behind(): return lax.ppermute(x, axis, [(i, (i + by) % count) for i in range(count)])]
    ppermute x7, starting transfers between devices: 8.97 us -> 10.2 us  [from_behind(): return lax.ppermute(x, axis, [(i, (i + by) % count) for i in range(count)])]
    reshape x1 -> x0, local copies, waits for them, and re-layouts: 1.01 us -> none  [on_device_shared(): pair_amps = amplitudes.reshape(pair_count, pno_count, pno_count)]
    unnamed x23 -> x27, local copies, waits for them, and re-layouts: 3.17 us -> 4.07 us
    ppermute x9, starting transfers between devices: 7.17 us -> 6.48 us  [from_partner(): lax.ppermute(x, axis, [(i, i ^ flip) for i in range(lax.axis_size(axis))])]
  transfers between devices with their start and end apart: 17 -> 17, of which waited for: 4 -> 5; matrix products, arithmetic and copies ran while one was open for 2% -> 0% of each run, Pallas kernels for 38% -> 39%
where the time goes in v1:
time: 55.2 us; the launch traced here: 54.9 us
  Pallas kernels  21.3 us (39%)
  starting transfers between devices  20.2 us (37%)
  waiting for transfers between devices  9.09 us (16%)
  local copies, waits for them, and re-layouts  4.07 us (7%)
    pallas_call x2, Pallas kernels, finish(): pl.pallas_call(lambda *refs: finish_kernel(members, group_count, len(piec...  10.6 us
    ppermute x7, starting transfers between devices, from_behind(): return lax.ppermute(x, axis, [(i, (i + by) % count) for i in range(count)])  10.2 us
    pallas_call x1, Pallas kernels, project(): pl.pallas_call(lambda *refs: project_kernel(len(bases), *refs), out_shape...  6.84 us
    ppermute x9, starting transfers between devices, from_partner(): lax.ppermute(x, axis, [(i, i ^ flip) for i in range(lax.axis_size(axis))])  6.48 us
    ppermute x7, waiting for transfers between devices, from_behind(): return lax.ppermute(x, axis, [(i, (i + by) % count) for i in range(count)])  4.75 us
    unnamed x27, local copies, waits for them, and re-layouts  4.07 us
    all_to_all x1, starting transfers between devices, on_device_shared(): lax.all_to_all(sent, 'blk', split_axis=0, concat_axis=0, tiled=True)  3.55 us
    all_to_all x1, waiting for transfers between devices, on_device_shared(): lax.all_to_all(sent, 'blk', split_axis=0, concat_axis=0, tiled=True)  3.08 us
  transfers between devices with their start and end apart: 17, of which 5 were waited for; matrix products, arithmetic and copies ran while one was open for 0% of the time, Pallas kernels for 39%

profile of v1, /device:TPU:0, one launch (start us, length us, event | category | flops | bytes accessed | tf_op | source)
XLA Modules:
  0.0 54.9 jit_solution(14913903293081536874)
XLA Ops:
  0.0 2.9 %collective-permute-start.2 = (f32[8,64,256]{2,1,0:T(8,128)}, f32[8,64,256]{2,1,0:T(8,128)S(1)}, u32[]{:S(2)}, u32[]{:S(2)}) collective-permute-start(f32[8,64,256]{2,1,0:T(8,128)} %refs_2_), channel_id=1, source_target_pairs={{0,8},{4,12},{8,0},{12,4},{16,24},{20,28},{24,16},{28,20},{1,9},{5... | collective-permute-start | bytes 1572872 | tf_op jit(solution)/shard_map/ppermute | solution.py:33
  2.9 1.5 %collective-permute-start = (f32[2,2,64,256]{3,2,1,0:T(8,128)}, f32[2,2,64,256]{3,2,1,0:T(8,128)S(1)}, u32[]{:S(2)}, u32[]{:S(2)}) collective-permute-start(f32[2,2,64,256]{3,2,1,0:T(8,128)} %refs_4_.1), channel_id=1, source_target_pairs={{0,16},{4,20},{8,24},{12,28},{16,0},{20,4},{24,8},{28,12},{1,17},{... | collective-permute-start | bytes 786440 | tf_op jit(solution)/shard_map/ppermute | solution.py:38
  4.5 1.6 %collective-permute-start.3 = (f32[2,2,64,256]{3,2,1,0:T(8,128)}, f32[2,2,64,256]{3,2,1,0:T(8,128)S(1)}, u32[]{:S(2)}, u32[]{:S(2)}) collective-permute-start(f32[2,2,64,256]{3,2,1,0:T(8,128)} %refs_4_.1), channel_id=1, source_target_pairs={{0,1},{1,2},{2,3},{3,0},{4,5},{5,6},{6,7},{7,4},{8,9},{9,10},{10,1... | collective-permute-start | bytes 786440 | tf_op jit(solution)/shard_map/ppermute | solution.py:38
  6.0 2.2 %collective-permute-start.4 = (f32[2,2,64,256]{3,2,1,0:T(8,128)}, f32[2,2,64,256]{3,2,1,0:T(8,128)S(1)}, u32[]{:S(2)}, u32[]{:S(2)}) collective-permute-start(f32[2,2,64,256]{3,2,1,0:T(8,128)} %refs_4_.1), channel_id=1, source_target_pairs={{0,3},{1,0},{2,1},{3,2},{4,7},{5,4},{6,5},{7,6},{8,11},{9,8},{10,9... | collective-permute-start | bytes 786440 | tf_op jit(solution)/shard_map/ppermute | solution.py:38
  8.3 1.0 %copy-done = f32[8,64,256]{2,1,0:T(8,128)S(1)} copy-done((f32[8,64,256]{2,1,0:T(8,128)S(1)}, f32[8,64,256]{2,1,0:T(8,128)}, u32[]{:S(2)}) %copy-start) | copy-done | bytes 524312
  9.3 0.9 %copy-done.2 = f32[8,4096]{1,0:T(8,128)S(1)} copy-done((f32[8,4096]{1,0:T(8,128)S(1)}, f32[8,4096]{1,0:T(8,128)}, u32[]{:S(2)}) %copy-start.2) | copy-done | bytes 131096
  10.2 0.7 %copy-done.4 = s32[1,1,8,1]{2,3,1,0:T(1,128)S(1)} copy-done((s32[1,1,8,1]{2,3,1,0:T(1,128)S(1)}, s32[1,1,8,1]{2,3,1,0:T(1,128)}, u32[]{:S(2)}) %copy-start.4) | copy-done | bytes 56
  10.9 0.0 copy-start.12
  10.9 1.5 %shard_map.73 = f32[8,80,256]{2,1,0:T(8,128)} custom-call(s32[8]{0:T(128)S(1)} %bitcast.6, f32[8,64,256]{2,1,0:T(8,128)S(1)} %copy-done, f32[8,4096]{1,0:T(8,128)S(1)} %copy-done.2), custom_call_target="tpu_custom_call" | custom-call | bytes 524288 | tf_op jit(solution)/shard_map/pallas_call | solution.py:64
  12.4 0.0 collective-permute-done.refs_4_
  12.4 3.6 %all-to-all-start = ((f32[8,80,256]{2,1,0:T(8,128)}), f32[8,80,256]{2,1,0:T(8,128)S(1)}, u32[]{:S(2)}, u32[]{:S(2)}) async-start(f32[8,80,256]{2,1,0:T(8,128)} %shard_map.73), calls=%async_computation | async-start | bytes 1310720 | tf_op jit(solution)/shard_map/all_to_all | solution.py:363
  16.0 0.0 copy-done.1
  16.0 0.0 copy-start.5
  16.0 0.4 collective-permute-start.1
  16.5 0.0 collective-permute-done.3.refs_5_
  16.5 2.6 %collective-permute-done.4.refs_7_ = f32[2,2,64,256]{3,2,1,0:T(8,128)S(1)} collective-permute-done((f32[2,2,64,256]{3,2,1,0:T(8,128)}, f32[2,2,64,256]{3,2,1,0:T(8,128)S(1)}, u32[]{:S(2)}, u32[]{:S(2)}) %collective-permute-start.4) | collective-permute-done | bytes 262176 | tf_op jit(solution)/shard_map/ppermute | solution.py:38
  19.1 0.7 %copy-done.8 = f32[2,2,64,256]{3,2,1,0:T(8,128)} copy-done((f32[2,2,64,256]{3,2,1,0:T(8,128)}, f32[2,2,64,256]{3,2,1,0:T(8,128)S(1)}, u32[]{:S(2)}) %copy-start.8) | copy-done | bytes 262168
  19.8 0.0 collective-permute-done.2.refs_2_
  19.8 0.0 collective-permute-start.5
  19.8 1.2 %collective-permute-start.6 = (f32[2,2,64,256]{3,2,1,0:T(8,128)}, f32[2,2,64,256]{3,2,1,0:T(8,128)}, u32[]{:S(2)}, u32[]{:S(2)}) collective-permute-start(f32[2,2,64,256]{3,2,1,0:T(8,128)} %copy-done.6), channel_id=1, source_target_pairs={{0,1},{1,2},{2,3},{3,0},{4,5},{5,6},{6,7},{7,4},{8,9},{9,10},{10,1... | collective-permute-start | bytes 786440 | tf_op jit(solution)/shard_map/ppermute | solution.py:38
  21.0 0.5 collective-permute-start.7
  21.5 2.7 %collective-permute-start.9 = (f32[2,2,64,256]{3,2,1,0:T(8,128)S(1)}, f32[2,2,64,256]{3,2,1,0:T(8,128)}, u32[]{:S(2)}, u32[]{:S(2)}) collective-permute-start(f32[2,2,64,256]{3,2,1,0:T(8,128)S(1)} %collective-permute-done.refs_4_), channel_id=1, source_target_pairs={{0,3},{1,0},{2,1},{3,2},{4,7},{5,4},{6,5},{7,6},{8,11},{9,8},{10,9... | collective-permute-start | bytes 786440 | tf_op jit(solution)/shard_map/ppermute | solution.py:38
  24.1 0.0 collective-permute-done.1.refs_1_.refs_3_
  24.1 3.1 %all-to-all-done.coupled = f32[8,80,256]{2,1,0:T(8,128)S(1)} async-done(((f32[8,80,256]{2,1,0:T(8,128)}), f32[8,80,256]{2,1,0:T(8,128)S(1)}, u32[]{:S(2)}, u32[]{:S(2)}) %all-to-all-start) | async-done | bytes 655392 | tf_op jit(solution)/shard_map/all_to_all | solution.py:363
  27.2 0.0 collective-permute-done.5.refs_3_
  27.2 2.3 %shard_map.74 = (f32[8,40,128]{2,1,0:T(8,128)S(1)}, f32[8,32,128]{2,1,0:T(8,128)S(1)}) custom-call(s32[8,8]{1,0:T(8,128)S(1)} %copy-done.10, f32[8,8]{1,0:T(8,128)S(1)} %copy-done.11, f32[8,16]{1,0:T(8,128)S(1)} %copy-done.12, f32[8,64,256]{2,1,0:T(8,128)S(1)} %copy-done.1, f32[8,4096]{1,0:T(8,128)S(1)} %copy-done.3, f32[8,80,256]{2,1,0:T(8,128)S(1)} %all-to-all-done.coupled), custom_call_target="tpu_custom_call" | custom-call | flops 4000000000 | bytes 1048576 | tf_op jit(solution)/shard_map/pallas_call | solution.py:124
  29.6 0.6 %collective-permute-start.10 = (f32[8,40,128]{2,1,0:T(8,128)S(1)}, f32[8,40,128]{2,1,0:T(8,128)S(1)}, u32[]{:S(2)}, u32[]{:S(2)}) collective-permute-start(f32[8,40,128]{2,1,0:T(8,128)S(1)} %get-tuple-element.44.refs_8_), channel_id=1, source_target_pairs={{0,8},{4,12},{8,0},{12,4},{16,24},{20,28},{24,16},{28,20},{1,9},{5... | collective-permute-start | bytes 491528 | tf_op jit(solution)/shard_map/ppermute | solution.py:33
  30.1 0.0 collective-permute-start.11
  30.1 0.9 %collective-permute-done.6.refs_6_ = f32[2,2,64,256]{3,2,1,0:T(8,128)} collective-permute-done((f32[2,2,64,256]{3,2,1,0:T(8,128)}, f32[2,2,64,256]{3,2,1,0:T(8,128)}, u32[]{:S(2)}, u32[]{:S(2)}) %collective-permute-start.6) | collective-permute-done | bytes 262176 | tf_op jit(solution)/shard_map/ppermute | solution.py:38
  31.0 0.5 collective-permute-start.8
  31.6 0.0 copy-done.7
  31.6 6.8 %shard_map.75 = (bf16[32,128,128]{2,1,0:T(8,128)(2,1)S(1)}, bf16[32,128,256]{2,1,0:T(8,128)(2,1)S(1)}) custom-call(f32[8,64,256]{2,1,0:T(8,128)S(1)} %copy-done.1, f32[8,64,256]{2,1,0:T(8,128)S(1)} %collective-permute-done.1.refs_1_.refs_3_, f32[8,64,256]{2,1,0:T(8,128)S(1)} %collective-permute-done.2.refs_2_, ...), custom_call_target="tpu_custom_call" | custom-call | flops 4026531840 | bytes 1048576 | tf_op jit(solution)/shard_map/pallas_call | solution.py:252
  38.4 0.0 collective-permute-done.7.refs_5_
  38.4 0.5 collective-permute-start.14
  39.0 0.0 collective-permute-done.9.refs_7_
  39.0 0.0 collective-permute-done.10.refs_8_
  39.0 0.0 collective-permute-done.11.refs_9_
  39.0 1.2 %collective-permute-done.8.refs_6_ = f32[2,2,64,256]{3,2,1,0:T(8,128)S(1)} collective-permute-done((f32[2,2,64,256]{3,2,1,0:T(8,128)}, f32[2,2,64,256]{3,2,1,0:T(8,128)S(1)}, u32[]{:S(2)}, u32[]{:S(2)}) %collective-permute-start.8) | collective-permute-done | bytes 262176 | tf_op jit(solution)/shard_map/ppermute | solution.py:38
  40.2 5.2 %shard_map.76 = (f32[8,32,128]{2,1,0:T(8,128)S(1)}, f32[8,32,128]{2,1,0:T(8,128)S(1)}) custom-call(bf16[32,128,128]{2,1,0:T(8,128)(2,1)S(1)} %get-tuple-element.49.refs_0_, bf16[32,128,256]{2,1,0:T(8,128)(2,1)S(1)} %get-tuple-element.50.refs_1_, f32[8,64,256]{2,1,0:T(8,128)S(1)} %collective-permute-done.2.refs_2_, ...), custom_call_target="tpu_custom_call" | custom-call | flops 2214592512 | bytes 1048576 | tf_op jit(solution)/shard_map/pallas_call | solution.py:324
  45.4 0.1 collective-permute-start.13
  45.5 1.5 %collective-permute-start.12 = (f32[8,32,128]{2,1,0:T(8,128)S(1)}, f32[8,32,128]{2,1,0:T(8,128)S(1)}, u32[]{:S(2)}, u32[]{:S(2)}) collective-permute-start(f32[8,32,128]{2,1,0:T(8,128)S(1)} %get-tuple-element.54), channel_id=1, source_target_pairs={{0,8},{4,12},{8,0},{12,4},{16,24},{20,28},{24,16},{28,20},{1,9},{5... | collective-permute-start | bytes 393224 | tf_op jit(solution)/shard_map/ppermute | solution.py:33
  47.0 0.0 collective-permute-done.14.refs_9_
  47.0 5.4 %shard_map.77 = (f32[8,32,128]{2,1,0:T(8,128)S(1)}, f32[8,32,128]{2,1,0:T(8,128)S(1)}) custom-call(bf16[32,128,128]{2,1,0:T(8,128)(2,1)S(1)} %get-tuple-element.49.refs_0_, bf16[32,128,256]{2,1,0:T(8,128)(2,1)S(1)} %get-tuple-element.50.refs_1_, f32[8,64,256]{2,1,0:T(8,128)S(1)} %copy-done.1, f32[8,64,256]{2,1,0:T(8,128)S(1)} %collective-permute-done.1.refs_1_.refs_3_, ...), custom_call_target="tpu_custom_call" | custom-call | flops 2214592512 | bytes 1048576 | tf_op jit(solution)/shard_map/pallas_call | solution.py:324
  52.4 0.4 collective-permute-start.15
  52.8 0.0 collective-permute-done.13
  52.9 1.2 %collective-permute-done.12 = f32[8,32,128]{2,1,0:T(8,128)S(1)} collective-permute-done((f32[8,32,128]{2,1,0:T(8,128)S(1)}, f32[8,32,128]{2,1,0:T(8,128)S(1)}, u32[]{:S(2)}, u32[]{:S(2)}) %collective-permute-start.12) | collective-permute-done | bytes 131104 | tf_op jit(solution)/shard_map/ppermute | solution.py:33
  54.1 0.0 collective-permute-done.15
  54.2 0.7 %copy.10 = f32[1,8,32,128]{3,1,2,0:T(8,128)} copy(f32[1,8,32,128]{3,2,1,0:T(8,128)S(1)} %add_bitcast_fusion) | data formatting | bytes 262144
  (20 shorter events, 0.1 us)
Async XLA Ops:
  0.0 19.8 %collective-permute-start.2 = (f32[8,64,256]{2,1,0:T(8,128)}, f32[8,64,256]{2,1,0:T(8,128)S(1)}, u32[]{:S(2)}, u32[]{:S(2)}) collective-permute-start(f32[8,64,256]{2,1,0:T(8,128)} %refs_2_), channel_id=1, source_target_pairs={{0,8},{4,12},{8,0},{12,4},{16,24},{20,28},{24,16},{28,20},{1,9},{5... | collective-permute-start | bytes 1572872 | tf_op jit(solution)/shard_map/ppermute | solution.py:33
  2.9 9.5 %collective-permute-start = (f32[2,2,64,256]{3,2,1,0:T(8,128)}, f32[2,2,64,256]{3,2,1,0:T(8,128)S(1)}, u32[]{:S(2)}, u32[]{:S(2)}) collective-permute-start(f32[2,2,64,256]{3,2,1,0:T(8,128)} %refs_4_.1), channel_id=1, source_target_pairs={{0,16},{4,20},{8,24},{12,28},{16,0},{20,4},{24,8},{28,12},{1,17},{... | collective-permute-start | bytes 786440 | tf_op jit(solution)/shard_map/ppermute | solution.py:38
  4.5 12.0 %collective-permute-start.3 = (f32[2,2,64,256]{3,2,1,0:T(8,128)}, f32[2,2,64,256]{3,2,1,0:T(8,128)S(1)}, u32[]{:S(2)}, u32[]{:S(2)}) collective-permute-start(f32[2,2,64,256]{3,2,1,0:T(8,128)} %refs_4_.1), channel_id=1, source_target_pairs={{0,1},{1,2},{2,3},{3,0},{4,5},{5,6},{6,7},{7,4},{8,9},{9,10},{10,1... | collective-permute-start | bytes 786440 | tf_op jit(solution)/shard_map/ppermute | solution.py:38
  6.0 13.0 %collective-permute-start.4 = (f32[2,2,64,256]{3,2,1,0:T(8,128)}, f32[2,2,64,256]{3,2,1,0:T(8,128)S(1)}, u32[]{:S(2)}, u32[]{:S(2)}) collective-permute-start(f32[2,2,64,256]{3,2,1,0:T(8,128)} %refs_4_.1), channel_id=1, source_target_pairs={{0,3},{1,0},{2,1},{3,2},{4,7},{5,4},{6,5},{7,6},{8,11},{9,8},{10,9... | collective-permute-start | bytes 786440 | tf_op jit(solution)/shard_map/ppermute | solution.py:38
  8.3 1.0 %copy-start = (f32[8,64,256]{2,1,0:T(8,128)S(1)}, f32[8,64,256]{2,1,0:T(8,128)}, u32[]{:S(2)}) copy-start(f32[8,64,256]{2,1,0:T(8,128)} %refs_2_) | copy-start | bytes 1572868
  9.3 0.9 %copy-start.2 = (f32[8,4096]{1,0:T(8,128)S(1)}, f32[8,4096]{1,0:T(8,128)}, u32[]{:S(2)}) copy-start(f32[8,4096]{1,0:T(8,128)} %amps.3) | copy-start | bytes 393220
  10.2 0.7 %copy-start.4 = (s32[1,1,8,1]{2,3,1,0:T(1,128)S(1)}, s32[1,1,8,1]{2,3,1,0:T(1,128)}, u32[]{:S(2)}) copy-start(s32[1,1,8,1]{2,3,1,0:T(1,128)} %param.9) | copy-start | bytes 100
  10.9 5.1 %copy-start.1 = (f32[8,64,256]{2,1,0:T(8,128)S(1)}, f32[8,64,256]{2,1,0:T(8,128)}, u32[]{:S(2)}) copy-start(f32[8,64,256]{2,1,0:T(8,128)} %refs_2_) | copy-start | bytes 1572868
  10.9 16.3 %copy-start.3 = (f32[8,4096]{1,0:T(8,128)S(1)}, f32[8,4096]{1,0:T(8,128)}, u32[]{:S(2)}) copy-start(f32[8,4096]{1,0:T(8,128)} %amps.3) | copy-start | bytes 393220
  10.9 16.3 %copy-start.10 = (s32[8,8]{1,0:T(8,128)S(1)}, s32[8,8]{1,0:T(8,128)}, u32[]{:S(2)}) copy-start(s32[8,8]{1,0:T(8,128)} %couple.1) | copy-start | bytes 772
  10.9 16.3 %copy-start.11 = (f32[8,8]{1,0:T(8,128)S(1)}, f32[8,8]{1,0:T(8,128)}, u32[]{:S(2)}) copy-start(f32[8,8]{1,0:T(8,128)} %couple_weight.1) | copy-start | bytes 772
  10.9 16.3 %copy-start.12 = (f32[8,16]{1,0:T(8,128)S(1)}, f32[8,16]{1,0:T(8,128)}, u32[]{:S(2)}) copy-start(f32[8,16]{1,0:T(8,128)} %fit_weight.1) | copy-start | bytes 1540
  12.4 14.7 %all-to-all-start = ((f32[8,80,256]{2,1,0:T(8,128)}), f32[8,80,256]{2,1,0:T(8,128)S(1)}, u32[]{:S(2)}, u32[]{:S(2)}) async-start(f32[8,80,256]{2,1,0:T(8,128)} %shard_map.73), calls=%async_computation | async-start | bytes 1310720 | tf_op jit(solution)/shard_map/all_to_all | solution.py:363
  16.0 15.5 %copy-start.5 = (f32[2,2,64,256]{3,2,1,0:T(8,128)S(1)}, f32[2,2,64,256]{3,2,1,0:T(8,128)}, u32[]{:S(2)}) copy-start(f32[2,2,64,256]{3,2,1,0:T(8,128)} %refs_4_.1) | copy-start | bytes 786436
  16.0 8.1 %collective-permute-start.1 = (f32[8,64,256]{2,1,0:T(8,128)S(1)}, f32[8,64,256]{2,1,0:T(8,128)S(1)}, u32[]{:S(2)}, u32[]{:S(2)}) collective-permute-start(f32[8,64,256]{2,1,0:T(8,128)S(1)} %copy-done.1), channel_id=1, source_target_pairs={{0,4},{4,0},{8,12},{12,8},{16,20},{20,16},{24,28},{28,24},{1,5},{5... | collective-permute-start | bytes 1572872 | tf_op jit(solution)/shard_map/ppermute | solution.py:33
  16.5 2.6 %copy-start.6 = (f32[2,2,64,256]{3,2,1,0:T(8,128)}, f32[2,2,64,256]{3,2,1,0:T(8,128)S(1)}, u32[]{:S(2)}) copy-start(f32[2,2,64,256]{3,2,1,0:T(8,128)S(1)} %collective-permute-done.3.refs_5_) | copy-start | bytes 786436
  19.1 0.7 %copy-start.8 = (f32[2,2,64,256]{3,2,1,0:T(8,128)}, f32[2,2,64,256]{3,2,1,0:T(8,128)S(1)}, u32[]{:S(2)}) copy-start(f32[2,2,64,256]{3,2,1,0:T(8,128)S(1)} %collective-permute-done.4.refs_7_) | copy-start | bytes 786436
  19.8 7.4 %collective-permute-start.5 = (f32[8,64,256]{2,1,0:T(8,128)S(1)}, f32[8,64,256]{2,1,0:T(8,128)S(1)}, u32[]{:S(2)}, u32[]{:S(2)}) collective-permute-start(f32[8,64,256]{2,1,0:T(8,128)S(1)} %collective-permute-done.2.refs_2_), channel_id=1, source_target_pairs={{0,4},{4,0},{8,12},{12,8},{16,20},{20,16},{24,28},{28,24},{1,5},{5... | collective-permute-start | bytes 1572872 | tf_op jit(solution)/shard_map/ppermute | solution.py:33
  19.8 11.3 %collective-permute-start.6 = (f32[2,2,64,256]{3,2,1,0:T(8,128)}, f32[2,2,64,256]{3,2,1,0:T(8,128)}, u32[]{:S(2)}, u32[]{:S(2)}) collective-permute-start(f32[2,2,64,256]{3,2,1,0:T(8,128)} %copy-done.6), channel_id=1, source_target_pairs={{0,1},{1,2},{2,3},{3,0},{4,5},{5,6},{6,7},{7,4},{8,9},{9,10},{10,1... | collective-permute-start | bytes 786440 | tf_op jit(solution)/shard_map/ppermute | solution.py:38
  21.0 17.4 %collective-permute-start.7 = (f32[2,2,64,256]{3,2,1,0:T(8,128)}, f32[2,2,64,256]{3,2,1,0:T(8,128)}, u32[]{:S(2)}, u32[]{:S(2)}) collective-permute-start(f32[2,2,64,256]{3,2,1,0:T(8,128)} %copy-done.6), channel_id=1, source_target_pairs={{0,16},{4,20},{8,24},{12,28},{16,0},{20,4},{24,8},{28,12},{1,17},{... | collective-permute-start | bytes 786440 | tf_op jit(solution)/shard_map/ppermute | solution.py:38
  21.5 17.5 %collective-permute-start.9 = (f32[2,2,64,256]{3,2,1,0:T(8,128)S(1)}, f32[2,2,64,256]{3,2,1,0:T(8,128)}, u32[]{:S(2)}, u32[]{:S(2)}) collective-permute-start(f32[2,2,64,256]{3,2,1,0:T(8,128)S(1)} %collective-permute-done.refs_4_), channel_id=1, source_target_pairs={{0,3},{1,0},{2,1},{3,2},{4,7},{5,4},{6,5},{7,6},{8,11},{9,8},{10,9... | collective-permute-start | bytes 786440 | tf_op jit(solution)/shard_map/ppermute | solution.py:38
  27.2 4.4 %copy-start.7 = (f32[2,2,64,256]{3,2,1,0:T(8,128)S(1)}, f32[2,2,64,256]{3,2,1,0:T(8,128)}, u32[]{:S(2)}) copy-start(f32[2,2,64,256]{3,2,1,0:T(8,128)} %copy-done.6) | copy-start | bytes 786436
  27.2 4.4 %copy-start.9 = (f32[2,2,64,256]{3,2,1,0:T(8,128)S(1)}, f32[2,2,64,256]{3,2,1,0:T(8,128)}, u32[]{:S(2)}) copy-start(f32[2,2,64,256]{3,2,1,0:T(8,128)} %copy-done.8) | copy-start | bytes 786436
  29.6 9.4 %collective-permute-start.10 = (f32[8,40,128]{2,1,0:T(8,128)S(1)}, f32[8,40,128]{2,1,0:T(8,128)S(1)}, u32[]{:S(2)}, u32[]{:S(2)}) collective-permute-start(f32[8,40,128]{2,1,0:T(8,128)S(1)} %get-tuple-element.44.refs_8_), channel_id=1, source_target_pairs={{0,8},{4,12},{8,0},{12,4},{16,24},{20,28},{24,16},{28,20},{1,9},{5... | collective-permute-start | bytes 491528 | tf_op jit(solution)/shard_map/ppermute | solution.py:33
  30.1 8.9 %collective-permute-start.11 = (f32[8,40,128]{2,1,0:T(8,128)S(1)}, f32[8,40,128]{2,1,0:T(8,128)S(1)}, u32[]{:S(2)}, u32[]{:S(2)}) collective-permute-start(f32[8,40,128]{2,1,0:T(8,128)S(1)} %get-tuple-element.44.refs_8_), channel_id=1, source_target_pairs={{0,12},{4,8},{8,4},{12,0},{16,28},{20,24},{24,20},{28,16},{1,13},{... | collective-permute-start | bytes 491528 | tf_op jit(solution)/shard_map/ppermute | solution.py:33
  31.0 9.1 %collective-permute-start.8 = (f32[2,2,64,256]{3,2,1,0:T(8,128)}, f32[2,2,64,256]{3,2,1,0:T(8,128)S(1)}, u32[]{:S(2)}, u32[]{:S(2)}) collective-permute-start(f32[2,2,64,256]{3,2,1,0:T(8,128)} %collective-permute-done.6.refs_6_), channel_id=1, source_target_pairs={{0,16},{4,20},{8,24},{12,28},{16,0},{20,4},{24,8},{28,12},{1,17},{... | collective-permute-start | bytes 786440 | tf_op jit(solution)/shard_map/ppermute | solution.py:38
  38.4 8.6 %collective-permute-start.14 = (f32[8,40,128]{2,1,0:T(8,128)S(1)}, f32[8,40,128]{2,1,0:T(8,128)S(1)}, u32[]{:S(2)}, u32[]{:S(2)}) collective-permute-start(f32[8,40,128]{2,1,0:T(8,128)S(1)} %get-tuple-element.44.refs_8_), channel_id=1, source_target_pairs={{0,4},{4,0},{8,12},{12,8},{16,20},{20,16},{24,28},{28,24},{1,5},{5... | collective-permute-start | bytes 491528 | tf_op jit(solution)/shard_map/ppermute | solution.py:33
  45.4 7.4 %collective-permute-start.13 = (f32[8,32,128]{2,1,0:T(8,128)S(1)}, f32[8,32,128]{2,1,0:T(8,128)S(1)}, u32[]{:S(2)}, u32[]{:S(2)}) collective-permute-start(f32[8,32,128]{2,1,0:T(8,128)S(1)} %get-tuple-element.55), channel_id=1, source_target_pairs={{0,12},{4,8},{8,4},{12,0},{16,28},{20,24},{24,20},{28,16},{1,13},{... | collective-permute-start | bytes 393224 | tf_op jit(solution)/shard_map/ppermute | solution.py:33
  45.5 8.6 %collective-permute-start.12 = (f32[8,32,128]{2,1,0:T(8,128)S(1)}, f32[8,32,128]{2,1,0:T(8,128)S(1)}, u32[]{:S(2)}, u32[]{:S(2)}) collective-permute-start(f32[8,32,128]{2,1,0:T(8,128)S(1)} %get-tuple-element.54), channel_id=1, source_target_pairs={{0,8},{4,12},{8,0},{12,4},{16,24},{20,28},{24,16},{28,20},{1,9},{5... | collective-permute-start | bytes 393224 | tf_op jit(solution)/shard_map/ppermute | solution.py:33
  52.4 1.7 %collective-permute-start.15 = (f32[8,32,128]{2,1,0:T(8,128)S(1)}, f32[8,32,128]{2,1,0:T(8,128)S(1)}, u32[]{:S(2)}, u32[]{:S(2)}) collective-permute-start(f32[8,32,128]{2,1,0:T(8,128)S(1)} %get-tuple-element.61), channel_id=1, source_target_pairs={{0,4},{4,0},{8,12},{12,8},{16,20},{20,16},{24,28},{28,24},{1,5},{5... | collective-permute-start | bytes 393224 | tf_op jit(solution)/shard_map/ppermute | solution.py:33
